TPU v7x, 32 devices: a whole 2x2x4 slice. The times are simulated.
32 devices in a mesh: member: 2 (over x), region: 4 (over y, core), sub: 4 (over z).
Axes of the slice: x: 2, y: 2, z: 4, core: 2. Of those that a mesh axis runs over, the one named last changes fastest.
Arguments:
- velocity: float32 [128, 16, 2, 48, 128], P(('member', 'region'), 'sub'), parts along dimension 0, may hold values from -6 to 6
- rbf_coef: float32 [64, 16, 16, 1152], P('region', 'sub'), may hold values from -0.1875 to 0.1875
- positions: float32 [8, 4, 3, 36864], P(('member', 'region'), 'sub'), parts along dimension 0, may hold values from 0 to 16, as said below
- cell_bins: int32 [8, 4, 36864], P(('member', 'region'), 'sub'), parts along dimension 0, may hold values from 0 to 63, as said below
- live_count: int32 [8, 4], P(('member', 'region'), 'sub'), parts along dimension 0, may hold values from 2176 to 34816, as said below
- departures: int32 [8, 4, 2, 8, 128], P(('member', 'region'), 'sub'), parts along dimension 0, may hold values from -1 to 36863, as said below
Outputs:
- final_positions: float32 [8, 4, 3, 36864], P(('member', 'region'), 'sub'), parts along dimension 0
There are 2 independent parts, one for each index of `member`. A program takes and returns all parts, laid end to end along the dimension named above; an argument that names none is the same for every part. Nothing has to cross between parts.
Inputs may be any that keep to these rules, and one draw needn't show every extreme that they name: `live_count`: one region's partitions hold exactly 34816 live particles, all others fewer; live slots are the first ones. `cell_bins`: A slot listed in departures lies in a block on the partition edge (or corner) facing its destination. `positions`: x and y lie within the slot's cell block, z between 1 and 14; a listed slot lies within 0.1 of the edge it crosses. `departures`: every listed slot is live at its substep, named once over both substeps and leaves toward a partition inside the grid; listed entries come first in each list, the rest are -1; some partition fills a list of 128 in every draw.
All inputs are finite; a program needn't handle non-finite values.
Results may differ from a plain program's by a relative error of at most 0.0003.
Values sent between devices are 32-bit elements; how exact they have to be, the bound alone decides.
A program may use at most 192 MiB of HBM per device.

v0:
```python
import functools
import jax
import jax.numpy as jnp
from jax import lax
from jax.experimental import pallas as pl
from jax.experimental.pallas import tpu as pltpu
from jax.sharding import PartitionSpec as P

L = 16
NB = 16
MIG = 128
LANES = 128
CHUNK = 512

time_step = 0.1
compass = ((-1, -1), (-1, 0), (-1, 1), (0, -1), (0, 1), (1, -1), (1, 0), (1, 1))

MESH = pl.DeviceIdType.MESH
f32 = jnp.float32
bf16 = jnp.bfloat16
VMEM_LIMIT = 48 * 2**20


def halves(v):
    hi = v.astype(bf16)
    return hi, (v - hi.astype(f32)).astype(bf16)


def thirds(v):
    hi = v.astype(bf16)
    rest = v - hi.astype(f32)
    mid = rest.astype(bf16)
    return hi, mid, (rest - mid.astype(f32)).astype(bf16)


def mm(a, b, ca, cb):
    return lax.dot_general(a, b, (((ca,), (cb,)), ((), ())), preferred_element_type=f32)


def hot_rows(rows, which):
    ids = lax.broadcasted_iota(jnp.int32, (rows, which.shape[1]), 0)
    return jnp.where(ids == which, 1.0, 0.0)


def velocity_at(x, y, z, ax, ay, hot, table):
    width = x.shape[1]
    centre = (lax.broadcasted_iota(jnp.int32, (4, width), 0).astype(f32) + 0.5) * 0.25
    dx = (x - ax) - centre
    dy = (y - ay) - centre
    phix = jnp.exp(dx * dx * (-1.0 / 0.18))
    phiy = jnp.exp(dy * dy * (-1.0 / 0.18))
    hi, lo = halves(phix)
    hi, lo = hi.astype(f32), lo.astype(f32)
    high, low = [], []
    for j in range(4):
        high.append(hot * jnp.broadcast_to(hi[j : j + 1], hot.shape).astype(bf16))
        low.append(hot * jnp.broadcast_to(lo[j : j + 1], hot.shape).astype(bf16))
    feats = jnp.concatenate(high + high + low, axis=0)
    s = mm(table, feats, 1, 0)
    t = s[0:48] * phiy[0:1]
    for j in range(1, 4):
        t = t + s[48 * j : 48 * j + 48] * phiy[j : j + 1]
    level = lax.broadcasted_iota(jnp.int32, (L, width), 0).astype(f32)
    hat = jnp.maximum(0.0, 1.0 - jnp.abs(z - level))
    return [jnp.sum(t[16 * c : 16 * c + 16] * hat, axis=0, keepdims=True) for c in range(3)]


def anchors(n, by):
    a = n // by
    return a.astype(f32), (n - a * by).astype(f32)


def gather_kernel(pos_ref, bins_ref, list_ref, listed_ref, gone_ref, rows):
    count = pos_ref.shape[1] // LANES
    padded = rows.shape[1]
    if padded > count:
        rows[:, count:, :] = jnp.zeros((4, padded - count, LANES), f32)

    def fold(q, carry):
        at = pl.ds(pl.multiple_of(q * LANES, LANES), LANES)
        v = pos_ref[:, at]
        for k in range(3):
            rows[k, pl.ds(q, 1), :] = v[k : k + 1]
        rows[3, pl.ds(q, 1), :] = bins_ref[:, at].astype(f32)
        return carry

    lax.fori_loop(0, count, fold, 0, unroll=8)
    slots = list_ref[...]
    hi_index = slots >> 7
    lo_index = jnp.where(slots >= 0, slots & 127, -1)
    hot_hi = hot_rows(padded, hi_index).astype(bf16)
    hot_lo = hot_rows(LANES, lo_index)
    gone_ref[...] = mm(hot_hi, hot_lo.astype(bf16), 1, 1)
    for k in range(4):
        turned = rows[k].T
        parts = thirds(turned) if k < 3 else (turned.astype(bf16),)
        y = mm(parts[0], hot_hi, 1, 0)
        for part in parts[1:]:
            y = y + mm(part, hot_hi, 1, 0)
        listed_ref[k : k + 1, :] = jnp.sum(y * hot_lo, axis=0, keepdims=True)


def coef_kernel(
    vel, west, east, north, south, cwest, ceast, rbf, listed, lists, tab, pay, fin, acc, tabf
):
    bx, by = vel.shape[0], vel.shape[1]
    blocks = bx * by
    acc[...] = jnp.zeros(acc.shape, f32)

    def row(source, targets):
        for j in range(-1, by + 1):
            v = source(j)
            vhi, vlo = halves(v)
            vcat = jnp.concatenate([vhi, vlo, vhi], axis=1)
            places, pieces = [], []
            for ti, u in targets:
                safe = jnp.clip(ti, 0, bx - 1)
                for tj in range(max(0, j - 1), min(by - 1, j + 1) + 1):
                    seg = 3 * (u + 1) + (j - tj + 1)
                    pieces.append(rbf[safe, tj, :, seg * 128 : (seg + 1) * 128])
                    places.append(((ti + 1) * by + tj) * NB)
            whi, wlo = halves(jnp.concatenate(pieces, axis=0))
            out = mm(jnp.concatenate([whi, whi, wlo], axis=1), vcat, 1, 1)
            for k, place in enumerate(places):
                at = pl.ds(pl.multiple_of(place, NB), NB)
                acc[at, :] += out[k * NB : (k + 1) * NB]

    def north_at(j):
        return cwest[0, 0] if j < 0 else ceast[0, 0] if j == by else north[0, j]

    def south_at(j):
        return cwest[1, 0] if j < 0 else ceast[1, 0] if j == by else south[0, j]

    row(north_at, [(jnp.int32(0), -1)])
    row(south_at, [(jnp.int32(bx - 1), 1)])

    def inner(i, carry):
        def at(j):
            return west[i, 0] if j < 0 else east[i, 0] if j == by else vel[i, j]

        row(at, [(i - 1, 1), (i, 0), (i + 1, -1)])
        return carry

    lax.fori_loop(0, bx, inner, 0)

    for jy in range(4):
        for pair in range(2):
            both = []
            for jx in (2 * pair, 2 * pair + 1):
                both.append(acc[pl.ds(by * NB + jx * 4 + jy, blocks, stride=NB), :])
            t = jnp.concatenate(both, axis=0).T
            columns = slice(pair * 2 * blocks, (pair + 1) * 2 * blocks)
            tabf[0, jy * 48 : jy * 48 + 48, columns] = t[0:48]
            tabf[1, jy * 48 : jy * 48 + 48, columns] = 0.5 * (t[0:48] + t[48:96])
    for m in range(2):
        hi, lo = halves(tabf[m])
        tab[m] = jnp.concatenate([hi, lo, hi], axis=1)

    per = CHUNK // MIG
    for c in range(lists.shape[1] // CHUNK):
        at = slice(c * CHUNK, (c + 1) * CHUNK)
        x, y, z = listed[0:1, at], listed[1:2, at], listed[2:3, at]
        n = (listed[3:4, at] + 0.5).astype(jnp.int32)
        flags = jnp.where(lists[:, at] >= 0, 1.0, 0.0)
        ax, ay = anchors(n, by)
        hot = hot_rows(blocks, n).astype(bf16)
        u = velocity_at(x, y, z, ax, ay, hot, tab[0])
        mx, my, mz = [p + 0.5 * time_step * q for p, q in zip((x, y, z), u)]
        first = c * per
        if first < 8:
            for k in range(per):
                d = first + k
                dr, dc = compass[d]
                sl = slice(k * MIG, (k + 1) * MIG)
                fl = flags[:, sl]
                na = jnp.clip(ax[:, sl] - float(dr * bx), 0.0, float(bx - 1))
                nb = jnp.clip(ay[:, sl] - float(dc * by), 0.0, float(by - 1))
                values = [
                    x[:, sl] - float(dr * bx), y[:, sl] - float(dc * by), z[:, sl],
                    mx[:, sl] - float(dr * bx), my[:, sl] - float(dc * by), mz[:, sl],
                    na * float(by) + nb,
                ]
                for r, v in enumerate(values):
                    pay[d, r : r + 1, :] = v * fl
                pay[d, 7:8, :] = fl
        else:
            u = velocity_at(mx, my, mz, ax, ay, hot, tab[1])
            there = slice((first - 8) * MIG, (first - 8 + per) * MIG)
            for k, (p, q) in enumerate(zip((x, y, z), u)):
                fin[k : k + 1, there] = p + time_step * q


def step_kernel(
    sizes, shape, split, live, pos, bins, gone, tab, pay, fin, leaving,
    out, land0, land1, box0, box1, pay1, spread, send0, recv0, send1, recv1,
):
    regions, subs = sizes
    bx, by = shape
    blocks = bx * by
    r, s = lax.axis_index("region"), lax.axis_index("sub")

    def present(d):
        a, b = r + compass[d][0], s + compass[d][1]
        return (a >= 0) & (a < regions) & (b >= 0) & (b < subs)

    def target(d):
        return {"region": r + compass[d][0], "sub": s + compass[d][1]}

    box0[...] = jnp.zeros(box0.shape, f32)
    box1[...] = jnp.zeros(box1.shape, f32)
    barrier = pltpu.get_barrier_semaphore()
    for d in range(8):
        @pl.when(present(d))
        def _():
            pl.semaphore_signal(barrier, inc=1, device_id=target(d), device_id_type=MESH)
    peers = jnp.int32(0)
    for d in range(8):
        peers = peers + jnp.where(present(d), 1, 0)
    pl.semaphore_wait(barrier, peers)

    def parcel(d, src, box, send, recv):
        return pltpu.make_async_remote_copy(
            src_ref=src.at[d], dst_ref=box.at[7 - d], send_sem=send.at[d],
            recv_sem=recv.at[7 - d], device_id=target(d), device_id_type=MESH,
        )

    def post(src, box, send, recv):
        for d in range(8):
            @pl.when(present(d))
            def _():
                parcel(d, src, box, send, recv).start()

    def collect(src, box, send, recv):
        for d in range(8):
            @pl.when(present(d))
            def _():
                parcel(d, src, box, send, recv).wait_send()
        for d in range(8):
            @pl.when(present(d))
            def _():
                parcel(7 - d, src, box, send, recv).wait_recv()

    resident = live[0, 0]

    def bulk(i, carry):
        at = pl.ds(pl.multiple_of(i * CHUNK, CHUNK), CHUNK)
        slot = lax.broadcasted_iota(jnp.int32, (1, CHUNK), 1) + i * CHUNK
        alive = slot < resident
        v = jnp.where(alive, pos[:, at], 0.0)
        x, y, z = v[0:1], v[1:2], v[2:3]
        n = bins[:, at]
        left = jnp.concatenate(
            [gone[pl.ds(i * (CHUNK // LANES) + k, 1), :] for k in range(CHUNK // LANES)], axis=1
        )
        ax, ay = anchors(n, by)
        hot = hot_rows(blocks, n).astype(bf16)
        u = velocity_at(x, y, z, ax, ay, hot, tab[0])
        mx, my, mz = [p + 0.5 * time_step * q for p, q in zip((x, y, z), u)]
        u = velocity_at(mx, my, mz, ax, ay, hot, tab[1])
        keep = alive & (left == 0.0)
        for k, (p, q) in enumerate(zip((x, y, z), u)):
            out[k : k + 1, at] = jnp.where(keep, p + time_step * q, 0.0)
        return carry

    post(pay, box0, send0, recv0)
    lax.fori_loop(0, split, bulk, 0)
    collect(pay, box0, send0, recv0)

    per = CHUNK // MIG
    living = []
    for c in range(8 // per):
        rows = [
            jnp.concatenate([box0[c * per + k, q : q + 1, :] for k in range(per)], axis=1)
            for q in range(8)
        ]
        n = (rows[6] + 0.5).astype(jnp.int32)
        ax, ay = anchors(n, by)
        hot = hot_rows(blocks, n).astype(bf16)
        u = velocity_at(rows[3], rows[4], rows[5], ax, ay, hot, tab[1])
        living.append(rows[7])
        for k in range(3):
            f = rows[k] + time_step * u[k]
            land0[k : k + 1, c * CHUNK : (c + 1) * CHUNK] = f
            for e in range(per):
                spread[c * per + e : c * per + e + 1, k * LANES : (k + 1) * LANES] = f[
                    :, e * LANES : (e + 1) * LANES
                ]

    slots = leaving[...]
    flags = jnp.where(slots >= 0, 1.0, 0.0)
    late = slots >= resident
    rel = jnp.where(late & (slots >= 0), slots - resident, -1)
    hot_hi = hot_rows(8, rel >> 7)
    hot_lo = hot_rows(LANES, jnp.where(rel >= 0, rel & 127, -1))
    hot_bf = jnp.concatenate([hot_hi, jnp.zeros(hot_hi.shape, f32)], axis=0).astype(bf16)
    left = mm(hot_bf, hot_lo.astype(bf16), 1, 1)
    wide = spread[...]
    wide = jnp.concatenate([wide, jnp.zeros(wide.shape, f32)], axis=0)
    picked = None
    for part in thirds(wide):
        y = mm(part, hot_bf, 0, 0)
        picked = y if picked is None else picked + y
    for k in range(3):
        mine = jnp.sum(picked[k * LANES : (k + 1) * LANES] * hot_lo, axis=0, keepdims=True)
        value = jnp.where(late, mine, fin[k : k + 1, :])
        for d in range(8):
            sl = slice(d * MIG, (d + 1) * MIG)
            shift = float((bx * compass[d][0], by * compass[d][1], 0)[k])
            pay1[d, k : k + 1, :] = (value[:, sl] - shift) * flags[:, sl]
    for d in range(8):
        pay1[d, 3:4, :] = flags[:, d * MIG : (d + 1) * MIG]
        pay1[d, 4:8, :] = jnp.zeros((4, MIG), f32)

    post(pay1, box1, send1, recv1)
    for d in range(8):
        sl = slice(d * MIG, (d + 1) * MIG)
        stays = jnp.where(left[d : d + 1] == 0.0, 1.0, 0.0)
        stays = stays * living[d // per][:, (d % per) * MIG : (d % per + 1) * MIG]
        land0[:, sl] = land0[:, sl] * stays
    lax.fori_loop(split, pos.shape[1] // CHUNK, bulk, 0)
    collect(pay1, box1, send1, recv1)
    for d in range(8):
        for k in range(3):
            land1[k : k + 1, d * MIG : (d + 1) * MIG] = box1[d, k : k + 1, :] * box1[d, 3:4, :]


def body(sizes, velocity, rbf_coef, positions, cell_bins, live_count, departures):
    bx, by, _, c3l, cb = velocity.shape
    cap = positions.shape[-1]
    count = 8 * MIG
    vel = velocity.reshape(bx, by, 2 * c3l, cb)
    rbf = rbf_coef
    pos = positions[0, 0]
    bins = cell_bins.reshape(1, cap)
    lists = departures.reshape(1, 2 * count)
    vmem = pl.BlockSpec(memory_space=pltpu.VMEM)
    smem = pl.BlockSpec(memory_space=pltpu.SMEM)
    local = pltpu.CompilerParams(vmem_limit_bytes=VMEM_LIMIT)

    def shift(block, axis, up):
        size = lax.axis_size(axis)
        pairs = [(i, i + 1) for i in range(size - 1)]
        return lax.ppermute(block, axis, pairs if up else [(b, a) for a, b in pairs])

    west = shift(vel[:, by - 1 :], "sub", True)
    east = shift(vel[:, :1], "sub", False)
    north = shift(vel[bx - 1 :], "region", True)
    south = shift(vel[:1], "region", False)
    cwest = shift(jnp.concatenate([north[:, by - 1 :], south[:, by - 1 :]], axis=0), "sub", True)
    ceast = shift(jnp.concatenate([north[:, :1], south[:, :1]], axis=0), "sub", False)

    rows = -(-(cap // LANES) // 128) * 128
    listed, gone = pl.pallas_call(
        gather_kernel,
        out_shape=(
            jax.ShapeDtypeStruct((4, 2 * count), f32),
            jax.ShapeDtypeStruct((rows, LANES), f32),
        ),
        in_specs=[vmem] * 3,
        out_specs=(vmem, vmem),
        scratch_shapes=[pltpu.VMEM((4, rows, LANES), f32)],
        compiler_params=local,
        cost_estimate=pl.CostEstimate(flops=4 * 10**9, bytes_accessed=10**6, transcendentals=0),
        name="gather_lists",
    )(pos, bins, lists)

    blocks = bx * by
    tab, pay, fin = pl.pallas_call(
        coef_kernel,
        out_shape=(
            jax.ShapeDtypeStruct((2, 192, 12 * blocks), bf16),
            jax.ShapeDtypeStruct((8, 8, MIG), f32),
            jax.ShapeDtypeStruct((3, count), f32),
        ),
        in_specs=[vmem] * 10,
        out_specs=(vmem,) * 3,
        scratch_shapes=[
            pltpu.VMEM(((bx + 2) * by * NB, 2 * c3l), f32),
            pltpu.VMEM((2, 192, 4 * blocks), f32),
        ],
        compiler_params=local,
        name="coefficients",
    )(vel, west, east, north, south, cwest, ceast, rbf, listed, lists)

    out, land0, land1 = pl.pallas_call(
        functools.partial(step_kernel, sizes, (bx, by), 20),
        out_shape=(
            jax.ShapeDtypeStruct((3, cap), f32),
            jax.ShapeDtypeStruct((3, count), f32),
            jax.ShapeDtypeStruct((3, count), f32),
        ),
        in_specs=[smem] + [vmem] * 7,
        out_specs=(vmem,) * 3,
        scratch_shapes=[
            pltpu.VMEM((8, 8, MIG), f32),
            pltpu.VMEM((8, 8, MIG), f32),
            pltpu.VMEM((8, 8, MIG), f32),
            pltpu.VMEM((8, 3 * LANES), f32),
            pltpu.SemaphoreType.DMA((8,)),
            pltpu.SemaphoreType.DMA((8,)),
            pltpu.SemaphoreType.DMA((8,)),
            pltpu.SemaphoreType.DMA((8,)),
        ],
        compiler_params=pltpu.CompilerParams(
            collective_id=0, has_side_effects=True, vmem_limit_bytes=VMEM_LIMIT
        ),
        name="advect",
    )(live_count, pos, bins, gone, tab, pay, fin, lists[:, count:])
    resident = live_count[0, 0]
    out = lax.dynamic_update_slice(out, land0, (jnp.int32(0), resident))
    out = lax.dynamic_update_slice(out, land1, (jnp.int32(0), resident + count))
    return out[None, None]


def solution(mesh):
    in_specs = (
        P(("member", "region"), "sub", None, None, None),
        P("region", "sub", None, None),
        P(("member", "region"), "sub", None, None),
        P(("member", "region"), "sub", None),
        P(("member", "region"), "sub"),
        P(("member", "region"), "sub", None, None, None),
    )
    out_specs = P(("member", "region"), "sub", None, None)
    sizes = (mesh.shape["region"], mesh.shape["sub"])
    return jax.shard_map(
        functools.partial(body, sizes), mesh=mesh, in_specs=in_specs, out_specs=out_specs,
        check_vma=False,
    )
```

profile of v0, /device:TPU:1, one launch (start us, length us, event | category | flops | bytes accessed | tf_op | source)
XLA Modules:
  0.0 105.5 jit_solution(10614299350382687046)
XLA Ops:
  0.0 0.0 copy-start.10
  0.0 0.0 copy-start.5
  0.0 0.0 copy-start.9
  0.0 1.1 %fusion = (f32[1,4,2,48,128]{4,3,2,1,0:T(8,128)S(1)}, f32[1,4,2,48,128]{4,3,2,1,0:T(8,128)S(1)}) fusion(f32[16,4,2,48,128]{4,3,2,1,0:T(8,128)} %param.6), kind=kLoop, calls=%fused_computation.3 | loop fusion | bytes 786432 | tf_op jit(solution)/shard_map/slice | solution.py:348
  1.1 2.0 %collective-permute-start.3 = (f32[1,4,96,128]{3,2,1,0:T(8,128)S(1)}, f32[1,4,96,128]{3,2,1,0:T(8,128)S(1)}, u32[]{:S(2)}, u32[]{:S(2)}) collective-permute-start(f32[1,4,96,128]{3,2,1,0:T(8,128)S(1)} %bitcast.30), channel_id=1, source_target_pairs={{4,0},{8,4},{12,8},{5,1},{9,5},{13,9},{6,2},{10,6},{14,10},{7,3},{... | collective-permute-start | bytes 589832 | tf_op jit(solution)/shard_map/ppermute | solution.py:343
  3.1 2.6 %fusion.1 = (f32[16,1,96,128]{3,2,1,0:T(8,128)}, f32[16,1,96,128]{3,2,1,0:T(8,128)}) fusion(f32[16,4,96,128]{3,2,1,0:T(8,128)} %bitcast.17), kind=kLoop, calls=%fused_computation.4 | loop fusion | bytes 3145728 | tf_op jit(solution)/shard_map/slice | solution.py:346
  5.7 5.5 %collective-permute-start = (f32[16,1,96,128]{3,2,1,0:T(8,128)}, f32[16,1,96,128]{3,2,1,0:T(8,128)}, u32[]{:S(2)}, u32[]{:S(2)}) collective-permute-start(f32[16,1,96,128]{3,2,1,0:T(8,128)} %get-tuple-element.24), channel_id=1, source_target_pairs={{0,1},{1,2},{2,3},{4,5},{5,6},{6,7},{8,9},{9,10},{10,11},{12,13},{... | collective-permute-start | bytes 2359304 | tf_op jit(solution)/shard_map/ppermute | solution.py:343
  11.3 1.3 %collective-permute-start.1 = (f32[16,1,96,128]{3,2,1,0:T(8,128)}, f32[16,1,96,128]{3,2,1,0:T(8,128)}, u32[]{:S(2)}, u32[]{:S(2)}) collective-permute-start(f32[16,1,96,128]{3,2,1,0:T(8,128)} %get-tuple-element.23), channel_id=1, source_target_pairs={{1,0},{2,1},{3,2},{5,4},{6,5},{7,6},{9,8},{10,9},{11,10},{13,12},{... | collective-permute-start | bytes 2359304 | tf_op jit(solution)/shard_map/ppermute | solution.py:343
  12.5 3.3 %collective-permute-start.2 = (f32[1,4,96,128]{3,2,1,0:T(8,128)S(1)}, f32[1,4,96,128]{3,2,1,0:T(8,128)S(1)}, u32[]{:S(2)}, u32[]{:S(2)}) collective-permute-start(f32[1,4,96,128]{3,2,1,0:T(8,128)S(1)} %bitcast.29), channel_id=1, source_target_pairs={{0,4},{4,8},{8,12},{1,5},{5,9},{9,13},{2,6},{6,10},{10,14},{3,7},{... | collective-permute-start | bytes 589832 | tf_op jit(solution)/shard_map/ppermute | solution.py:343
  15.9 0.0 copy-done.10
  15.9 0.3 copy.10
  16.2 0.0 copy-start.1
  16.2 0.0 collective-permute-done.3.south
  16.2 2.2 %collective-permute-done.2.north = f32[1,4,96,128]{3,2,1,0:T(8,128)S(1)} collective-permute-done((f32[1,4,96,128]{3,2,1,0:T(8,128)S(1)}, f32[1,4,96,128]{3,2,1,0:T(8,128)S(1)}, u32[]{:S(2)}, u32[]{:S(2)}) %collective-permute-start.2) | collective-permute-done | bytes 196640 | tf_op jit(solution)/shard_map/ppermute | solution.py:343
  18.5 0.6 pad_maximum_fusion
  19.1 4.9 %collective-permute-start.4 = (f32[2,1,96,128]{3,2,1,0:T(8,128)}, f32[2,1,96,128]{3,2,1,0:T(8,128)}, u32[]{:S(2)}, u32[]{:S(2)}) collective-permute-start(f32[2,1,96,128]{3,2,1,0:T(8,128)} %pad_maximum_fusion), channel_id=1, source_target_pairs={{0,1},{1,2},{2,3},{4,5},{5,6},{6,7},{8,9},{9,10},{10,11},{12,13},{... | collective-permute-start | bytes 294920 | tf_op jit(solution)/shard_map/ppermute | solution.py:343
  24.0 0.6 pad_maximum_fusion.1
  24.6 1.3 %collective-permute-start.5 = (f32[2,1,96,128]{3,2,1,0:T(8,128)}, f32[2,1,96,128]{3,2,1,0:T(8,128)}, u32[]{:S(2)}, u32[]{:S(2)}) collective-permute-start(f32[2,1,96,128]{3,2,1,0:T(8,128)} %pad_maximum_fusion.1), channel_id=1, source_target_pairs={{1,0},{2,1},{3,2},{5,4},{6,5},{7,6},{9,8},{10,9},{11,10},{13,12},{... | collective-permute-start | bytes 294920 | tf_op jit(solution)/shard_map/ppermute | solution.py:343
  25.9 0.0 copy-done.5
  25.9 0.0 copy-done.9
  25.9 0.0 copy-start
  26.0 4.1 %gather_lists.1 = (f32[4,2048]{1,0:T(4,128)S(1)}, f32[384,128]{1,0:T(8,128)S(1)}) custom-call(f32[3,36864]{1,0:T(4,128)S(1)} %bitcast.19, s32[1,36864]{1,0:T(1,128)S(1)} %bitcast.22, s32[1,2048]{1,0:T(1,128)S(1)} %bitcast.24), custom_call_target="tpu_custom_call" | custom-call | flops 4000000000 | bytes 1000000 | tf_op jit(solution)/shard_map/gather_lists/pallas_call | solution.py:353
  30.0 0.0 copy-done.1
  30.0 0.0 copy-start.3
  30.0 0.7 copy-done.3
  30.7 0.0 copy-start.7
  30.7 0.6 copy-done.7
  32.0 0.0 collective-permute-done.4.cwest
  32.0 3.0 %collective-permute-done.5.ceast = f32[2,1,96,128]{3,2,1,0:T(8,128)} collective-permute-done((f32[2,1,96,128]{3,2,1,0:T(8,128)}, f32[2,1,96,128]{3,2,1,0:T(8,128)}, u32[]{:S(2)}, u32[]{:S(2)}) %collective-permute-start.5) | collective-permute-done | bytes 98336 | tf_op jit(solution)/shard_map/ppermute | solution.py:343
  35.0 0.0 collective-permute-done.west
  35.0 0.0 collective-permute-done.1.east
  35.0 0.0 copy-done
  35.0 0.0 copy-start.8
  35.0 0.7 copy-done.8
  35.8 0.0 copy-start.2
  35.8 0.0 copy-start.4
  35.8 0.0 copy-start.6
  35.8 10.9 %coefficients.1 = (bf16[2,192,768]{2,1,0:T(8,128)(2,1)S(1)}, f32[8,8,128]{2,1,0:T(8,128)S(1)}, f32[3,1024]{1,0:T(4,128)S(1)}) custom-call(f32[16,4,96,128]{3,2,1,0:T(8,128)S(1)} %bitcast.18, f32[16,1,96,128]{3,2,1,0:T(8,128)} %collective-permute-done.west, f32[16,1,96,128]{3,2,1,0:T(8,128)} %collective-permute-done.1.east, ...), custom_call_target="tpu_custom_call" | custom-call | tf_op jit(solution)/shard_map/coefficients/pallas_call | solution.py:368
  46.6 0.0 copy-done.2
  46.7 0.0 copy-done.4
  46.7 0.0 copy-done.6
  46.7 56.6 %advect.1 = (f32[3,36864]{1,0:T(4,128)S(1)}, f32[3,1024]{1,0:T(4,128)S(1)}, f32[3,1024]{1,0:T(4,128)S(1)}) custom-call(s32[1,1]{1,0:T(1,128)} %copy.13.live, f32[3,36864]{1,0:T(4,128)S(1)} %bitcast.20, s32[1,36864]{1,0:T(1,128)S(1)} %bitcast.23, f32[384,128]{1,0:T(8,128)S(1)} %copy-done.4, bf16[2,192,768]{2,1,0:T(8,128)(2,1)S(1)} %get-tuple-element.15.tab, ...), custom_call_target="tpu_custom_call" | custom-call | tf_op jit(solution)/shard_map/advect/pallas_call | solution.py:385
  103.2 0.5 dynamic_update_slice.8
  103.8 0.5 dynamic_update_slice.9
  104.3 1.2 %copy.7 = f32[1,1,3,36864]{3,1,2,0:T(1,128)} copy(f32[1,1,3,36864]{3,2,1,0:T(4,128)S(1)} %dynamic_update_slice.9) | data formatting | bytes 884736 | tf_op jit(solution)/shard_map/dynamic_update_slice | solution.py:411
  (3 shorter events, 0.0 us)
Async XLA Ops:
  0.0 15.9 %copy-start.10 = (f32[1,1,3,36864]{3,1,2,0:T(1,128)S(1)}, f32[1,1,3,36864]{3,1,2,0:T(1,128)}, u32[]{:S(2)}) copy-start(f32[1,1,3,36864]{3,1,2,0:T(1,128)} %param.8) | copy-start | bytes 1327108
  0.0 25.9 %copy-start.5 = (s32[1,1,36864]{2,1,0:T(1,128)S(1)}, s32[1,1,36864]{2,1,0:T(1,128)}, u32[]{:S(2)}) copy-start(s32[1,1,36864]{2,1,0:T(1,128)} %param.9) | copy-start | bytes 442372
  0.0 25.9 %copy-start.9 = (s32[1,1,2,8,128]{4,3,2,1,0:T(8,128)S(1)}, s32[1,1,2,8,128]{4,3,2,1,0:T(8,128)}, u32[]{:S(2)}) copy-start(s32[1,1,2,8,128]{4,3,2,1,0:T(8,128)} %param.11) | copy-start | bytes 24580
  1.1 15.1 %collective-permute-start.3 = (f32[1,4,96,128]{3,2,1,0:T(8,128)S(1)}, f32[1,4,96,128]{3,2,1,0:T(8,128)S(1)}, u32[]{:S(2)}, u32[]{:S(2)}) collective-permute-start(f32[1,4,96,128]{3,2,1,0:T(8,128)S(1)} %bitcast.30), channel_id=1, source_target_pairs={{4,0},{8,4},{12,8},{5,1},{9,5},{13,9},{6,2},{10,6},{14,10},{7,3},{... | collective-permute-start | bytes 589832 | tf_op jit(solution)/shard_map/ppermute | solution.py:343
  5.7 29.3 %collective-permute-start = (f32[16,1,96,128]{3,2,1,0:T(8,128)}, f32[16,1,96,128]{3,2,1,0:T(8,128)}, u32[]{:S(2)}, u32[]{:S(2)}) collective-permute-start(f32[16,1,96,128]{3,2,1,0:T(8,128)} %get-tuple-element.24), channel_id=1, source_target_pairs={{0,1},{1,2},{2,3},{4,5},{5,6},{6,7},{8,9},{9,10},{10,11},{12,13},{... | collective-permute-start | bytes 2359304 | tf_op jit(solution)/shard_map/ppermute | solution.py:343
  11.3 23.7 %collective-permute-start.1 = (f32[16,1,96,128]{3,2,1,0:T(8,128)}, f32[16,1,96,128]{3,2,1,0:T(8,128)}, u32[]{:S(2)}, u32[]{:S(2)}) collective-permute-start(f32[16,1,96,128]{3,2,1,0:T(8,128)} %get-tuple-element.23), channel_id=1, source_target_pairs={{1,0},{2,1},{3,2},{5,4},{6,5},{7,6},{9,8},{10,9},{11,10},{13,12},{... | collective-permute-start | bytes 2359304 | tf_op jit(solution)/shard_map/ppermute | solution.py:343
  12.5 5.9 %collective-permute-start.2 = (f32[1,4,96,128]{3,2,1,0:T(8,128)S(1)}, f32[1,4,96,128]{3,2,1,0:T(8,128)S(1)}, u32[]{:S(2)}, u32[]{:S(2)}) collective-permute-start(f32[1,4,96,128]{3,2,1,0:T(8,128)S(1)} %bitcast.29), channel_id=1, source_target_pairs={{0,4},{4,8},{8,12},{1,5},{5,9},{9,13},{2,6},{6,10},{10,14},{3,7},{... | collective-permute-start | bytes 589832 | tf_op jit(solution)/shard_map/ppermute | solution.py:343
  16.2 13.8 %copy-start.1 = (f32[1,1,3,36864]{3,2,1,0:T(4,128)}, f32[1,1,3,36864]{3,2,1,0:T(4,128)S(1)}, u32[]{:S(2)}) copy-start(f32[1,1,3,36864]{3,2,1,0:T(4,128)S(1)} %copy.10) | copy-start | bytes 1327108
  19.1 12.9 %collective-permute-start.4 = (f32[2,1,96,128]{3,2,1,0:T(8,128)}, f32[2,1,96,128]{3,2,1,0:T(8,128)}, u32[]{:S(2)}, u32[]{:S(2)}) collective-permute-start(f32[2,1,96,128]{3,2,1,0:T(8,128)} %pad_maximum_fusion), channel_id=1, source_target_pairs={{0,1},{1,2},{2,3},{4,5},{5,6},{6,7},{8,9},{9,10},{10,11},{12,13},{... | collective-permute-start | bytes 294920 | tf_op jit(solution)/shard_map/ppermute | solution.py:343
  24.6 10.4 %collective-permute-start.5 = (f32[2,1,96,128]{3,2,1,0:T(8,128)}, f32[2,1,96,128]{3,2,1,0:T(8,128)}, u32[]{:S(2)}, u32[]{:S(2)}) collective-permute-start(f32[2,1,96,128]{3,2,1,0:T(8,128)} %pad_maximum_fusion.1), channel_id=1, source_target_pairs={{1,0},{2,1},{3,2},{5,4},{6,5},{7,6},{9,8},{10,9},{11,10},{13,12},{... | collective-permute-start | bytes 294920 | tf_op jit(solution)/shard_map/ppermute | solution.py:343
  25.9 9.1 %copy-start = (f32[16,4,2,48,128]{4,3,2,1,0:T(8,128)S(1)}, f32[16,4,2,48,128]{4,3,2,1,0:T(8,128)}, u32[]{:S(2)}) copy-start(f32[16,4,2,48,128]{4,3,2,1,0:T(8,128)} %param.6) | copy-start | bytes 9437188
  30.0 0.7 copy-start.3
  30.7 0.6 copy-start.7
  35.0 0.8 copy-start.8
  35.8 10.9 %copy-start.2 = (f32[1,1,3,36864]{3,2,1,0:T(4,128)S(1)}, f32[1,1,3,36864]{3,2,1,0:T(4,128)}, u32[]{:S(2)}) copy-start(f32[1,1,3,36864]{3,2,1,0:T(4,128)} %copy-done.1) | copy-start | bytes 1327108
  35.8 10.9 %copy-start.4 = (f32[384,128]{1,0:T(8,128)S(1)}, f32[384,128]{1,0:T(8,128)}, u32[]{:S(2)}) copy-start(f32[384,128]{1,0:T(8,128)} %copy-done.3) | copy-start | bytes 589828
  35.8 10.9 %copy-start.6 = (s32[1,1,36864]{2,1,0:T(1,128)S(1)}, s32[1,1,36864]{2,1,0:T(1,128)}, u32[]{:S(2)}) copy-start(s32[1,1,36864]{2,1,0:T(1,128)} %param.9) | copy-start | bytes 442372
where the time goes:
time: 106 us; the launch traced here: 105 us
  Pallas kernels  71.5 us (67%)
  starting transfers between devices  18.3 us (17%)
  local copies, waits for them, and re-layouts  8.32 us (8%)
  waiting for transfers between devices  5.25 us (5%)
  other arithmetic  1.27 us (1%)
    pallas_call x1, Pallas kernels, body(): pl.pallas_call(functools.partial(step_kernel, sizes, (bx, by), 20), out_s...  56.6 us
    ppermute x6, starting transfers between devices, shift(): lax.ppermute(block, axis, pairs if up else [(b, a) for a, b in pairs])  18.3 us
    pallas_call x1, Pallas kernels, body(): pl.pallas_call(coef_kernel, out_shape=(jax.ShapeDtypeStruct((2, 192, 12 *...  10.9 us
    ppermute x6, waiting for transfers between devices, shift(): lax.ppermute(block, axis, pairs if up else [(b, a) for a, b in pairs])  5.25 us
    pallas_call x1, Pallas kernels, body(): pl.pallas_call(gather_kernel, out_shape=(jax.ShapeDtypeStruct((4, 2 * cou...  4.07 us
    slice x1, local copies, waits for them, and re-layouts, body(): east = shift(vel[:, :1], 'sub', False)  2.62 us
    unnamed x23, local copies, waits for them, and re-layouts  2.36 us
  transfers between devices with their start and end apart: 6, of which 2 were waited for; matrix products, arithmetic and copies ran while one was open for 4% of the time, Pallas kernels for 4%

commit v1 on v0

--- a/solution.py
+++ b/solution.py
@@ -10,7 +10,8 @@
 NB = 16
 MIG = 128
 LANES = 128
-CHUNK = 512
+CHUNK = 1024
+BULK = 4096
 
 time_step = 0.1
 compass = ((-1, -1), (-1, 0), (-1, 1), (0, -1), (0, 1), (1, -1), (1, 0), (1, 1))
@@ -70,7 +71,7 @@
     return a.astype(f32), (n - a * by).astype(f32)
 
 
-def gather_kernel(pos_ref, bins_ref, list_ref, listed_ref, gone_ref, rows):
+def gather_lists(pos_ref, bins_ref, list_ref, listed_ref, gone_ref, rows):
     count = pos_ref.shape[1] // LANES
     padded = rows.shape[1]
     if padded > count:
@@ -100,15 +101,69 @@
         listed_ref[k : k + 1, :] = jnp.sum(y * hot_lo, axis=0, keepdims=True)
 
 
+def grid_peers(sizes):
+    regions, subs = sizes
+    r, s = lax.axis_index("region"), lax.axis_index("sub")
+
+    def present(d):
+        a, b = r + compass[d][0], s + compass[d][1]
+        return (a >= 0) & (a < regions) & (b >= 0) & (b < subs)
+
+    def target(d):
+        return {"region": r + compass[d][0], "sub": s + compass[d][1]}
+
+    return present, target
+
+
+def greet(present, target):
+    barrier = pltpu.get_barrier_semaphore()
+    peers = jnp.int32(0)
+    for d in range(8):
+        peers = peers + jnp.where(present(d), 1, 0)
+
+        @pl.when(present(d))
+        def _():
+            pl.semaphore_signal(barrier, inc=1, device_id=target(d), device_id_type=MESH)
+    pl.semaphore_wait(barrier, peers)
+
+
 def coef_kernel(
-    vel, west, east, north, south, cwest, ceast, rbf, listed, lists, tab, pay, fin, acc, tabf
+    sizes, vel, rbf, pos, bins, lists, tab, pay, fin, gone,
+    west, east, north, south, corners, acc, tabf, listed, folded, send, recv,
 ):
     bx, by = vel.shape[0], vel.shape[1]
     blocks = bx * by
+    present, target = grid_peers(sizes)
+    for box in (west, east, north, south, corners):
+        box[...] = jnp.zeros(box.shape, f32)
+    greet(present, target)
+    boxes = [corners.at[0], north, corners.at[1], west, east, corners.at[2], south, corners.at[3]]
+
+    def halo(e):
+        dr, dc = compass[e]
+        row_at = 0 if dr < 0 else bx - 1
+        col_at = 0 if dc < 0 else by - 1
+        if dr == 0:
+            src = vel.at[:, col_at]
+        elif dc == 0:
+            src = vel.at[row_at]
+        else:
+            src = vel.at[row_at, col_at]
+        return pltpu.make_async_remote_copy(
+            src_ref=src, dst_ref=boxes[7 - e], send_sem=send.at[e], recv_sem=recv.at[7 - e],
+            device_id=target(e), device_id_type=MESH,
+        )
+
+    for e in (3, 4, 0, 2, 5, 7, 1, 6):
+        @pl.when(present(e))
+        def _():
+            halo(e).start()
+
+    gather_lists(pos, bins, lists, listed, gone, folded)
     acc[...] = jnp.zeros(acc.shape, f32)
 
-    def row(source, targets):
-        for j in range(-1, by + 1):
+    def row(source, targets, columns):
+        for j in columns:
             v = source(j)
             vhi, vlo = halves(v)
             vcat = jnp.concatenate([vhi, vlo, vhi], axis=1)
@@ -126,22 +181,34 @@
                 acc[at, :] += out[k * NB : (k + 1) * NB]
 
     def north_at(j):
-        return cwest[0, 0] if j < 0 else ceast[0, 0] if j == by else north[0, j]
+        return corners[0] if j < 0 else corners[1] if j == by else north[j]
 
     def south_at(j):
-        return cwest[1, 0] if j < 0 else ceast[1, 0] if j == by else south[0, j]
-
-    row(north_at, [(jnp.int32(0), -1)])
-    row(south_at, [(jnp.int32(bx - 1), 1)])
+        return corners[2] if j < 0 else corners[3] if j == by else south[j]
+
+    def around(i):
+        return [(i - 1, 1), (i, 0), (i + 1, -1)]
 
     def inner(i, carry):
-        def at(j):
-            return west[i, 0] if j < 0 else east[i, 0] if j == by else vel[i, j]
-
-        row(at, [(i - 1, 1), (i, 0), (i + 1, -1)])
+        row(lambda j: vel[i, j], around(i), range(by))
         return carry
 
+    def outer(i, carry):
+        row(lambda j: west[i] if j < 0 else east[i], around(i), (-1, by))
+        return carry
+
     lax.fori_loop(0, bx, inner, 0)
+    for e in range(8):
+        @pl.when(present(e))
+        def _():
+            halo(e).wait_send()
+    for e in range(8):
+        @pl.when(present(e))
+        def _():
+            halo(7 - e).wait_recv()
+    row(north_at, [(jnp.int32(0), -1)], range(-1, by + 1))
+    row(south_at, [(jnp.int32(bx - 1), 1)], range(-1, by + 1))
+    lax.fori_loop(0, bx, outer, 0)
 
     for jy in range(4):
         for pair in range(2):
@@ -194,29 +261,12 @@
     sizes, shape, split, live, pos, bins, gone, tab, pay, fin, leaving,
     out, land0, land1, box0, box1, pay1, spread, send0, recv0, send1, recv1,
 ):
-    regions, subs = sizes
     bx, by = shape
     blocks = bx * by
-    r, s = lax.axis_index("region"), lax.axis_index("sub")
-
-    def present(d):
-        a, b = r + compass[d][0], s + compass[d][1]
-        return (a >= 0) & (a < regions) & (b >= 0) & (b < subs)
-
-    def target(d):
-        return {"region": r + compass[d][0], "sub": s + compass[d][1]}
-
+    present, target = grid_peers(sizes)
     box0[...] = jnp.zeros(box0.shape, f32)
     box1[...] = jnp.zeros(box1.shape, f32)
-    barrier = pltpu.get_barrier_semaphore()
-    for d in range(8):
-        @pl.when(present(d))
-        def _():
-            pl.semaphore_signal(barrier, inc=1, device_id=target(d), device_id_type=MESH)
-    peers = jnp.int32(0)
-    for d in range(8):
-        peers = peers + jnp.where(present(d), 1, 0)
-    pl.semaphore_wait(barrier, peers)
+    greet(present, target)
 
     def parcel(d, src, box, send, recv):
         return pltpu.make_async_remote_copy(
@@ -243,14 +293,14 @@
     resident = live[0, 0]
 
     def bulk(i, carry):
-        at = pl.ds(pl.multiple_of(i * CHUNK, CHUNK), CHUNK)
-        slot = lax.broadcasted_iota(jnp.int32, (1, CHUNK), 1) + i * CHUNK
+        at = pl.ds(pl.multiple_of(i * BULK, BULK), BULK)
+        slot = lax.broadcasted_iota(jnp.int32, (1, BULK), 1) + i * BULK
         alive = slot < resident
         v = jnp.where(alive, pos[:, at], 0.0)
         x, y, z = v[0:1], v[1:2], v[2:3]
         n = bins[:, at]
         left = jnp.concatenate(
-            [gone[pl.ds(i * (CHUNK // LANES) + k, 1), :] for k in range(CHUNK // LANES)], axis=1
+            [gone[pl.ds(i * (BULK // LANES) + k, 1), :] for k in range(BULK // LANES)], axis=1
         )
         ax, ay = anchors(n, by)
         hot = hot_rows(blocks, n).astype(bf16)
@@ -317,7 +367,7 @@
         stays = jnp.where(left[d : d + 1] == 0.0, 1.0, 0.0)
         stays = stays * living[d // per][:, (d % per) * MIG : (d % per + 1) * MIG]
         land0[:, sl] = land0[:, sl] * stays
-    lax.fori_loop(split, pos.shape[1] // CHUNK, bulk, 0)
+    lax.fori_loop(split, pos.shape[1] // BULK, bulk, 0)
     collect(pay1, box1, send1, recv1)
     for d in range(8):
         for k in range(3):
@@ -335,55 +385,39 @@
     lists = departures.reshape(1, 2 * count)
     vmem = pl.BlockSpec(memory_space=pltpu.VMEM)
     smem = pl.BlockSpec(memory_space=pltpu.SMEM)
-    local = pltpu.CompilerParams(vmem_limit_bytes=VMEM_LIMIT)
-
-    def shift(block, axis, up):
-        size = lax.axis_size(axis)
-        pairs = [(i, i + 1) for i in range(size - 1)]
-        return lax.ppermute(block, axis, pairs if up else [(b, a) for a, b in pairs])
-
-    west = shift(vel[:, by - 1 :], "sub", True)
-    east = shift(vel[:, :1], "sub", False)
-    north = shift(vel[bx - 1 :], "region", True)
-    south = shift(vel[:1], "region", False)
-    cwest = shift(jnp.concatenate([north[:, by - 1 :], south[:, by - 1 :]], axis=0), "sub", True)
-    ceast = shift(jnp.concatenate([north[:, :1], south[:, :1]], axis=0), "sub", False)
-
     rows = -(-(cap // LANES) // 128) * 128
-    listed, gone = pl.pallas_call(
-        gather_kernel,
-        out_shape=(
-            jax.ShapeDtypeStruct((4, 2 * count), f32),
-            jax.ShapeDtypeStruct((rows, LANES), f32),
-        ),
-        in_specs=[vmem] * 3,
-        out_specs=(vmem, vmem),
-        scratch_shapes=[pltpu.VMEM((4, rows, LANES), f32)],
-        compiler_params=local,
-        cost_estimate=pl.CostEstimate(flops=4 * 10**9, bytes_accessed=10**6, transcendentals=0),
-        name="gather_lists",
-    )(pos, bins, lists)
-
     blocks = bx * by
-    tab, pay, fin = pl.pallas_call(
-        coef_kernel,
+    tab, pay, fin, gone = pl.pallas_call(
+        functools.partial(coef_kernel, sizes),
         out_shape=(
             jax.ShapeDtypeStruct((2, 192, 12 * blocks), bf16),
             jax.ShapeDtypeStruct((8, 8, MIG), f32),
             jax.ShapeDtypeStruct((3, count), f32),
+            jax.ShapeDtypeStruct((rows, LANES), f32),
         ),
-        in_specs=[vmem] * 10,
-        out_specs=(vmem,) * 3,
+        in_specs=[vmem] * 5,
+        out_specs=(vmem,) * 4,
         scratch_shapes=[
+            pltpu.VMEM((bx, 2 * c3l, cb), f32),
+            pltpu.VMEM((bx, 2 * c3l, cb), f32),
+            pltpu.VMEM((by, 2 * c3l, cb), f32),
+            pltpu.VMEM((by, 2 * c3l, cb), f32),
+            pltpu.VMEM((4, 2 * c3l, cb), f32),
             pltpu.VMEM(((bx + 2) * by * NB, 2 * c3l), f32),
             pltpu.VMEM((2, 192, 4 * blocks), f32),
+            pltpu.VMEM((4, 2 * count), f32),
+            pltpu.VMEM((4, rows, LANES), f32),
+            pltpu.SemaphoreType.DMA((8,)),
+            pltpu.SemaphoreType.DMA((8,)),
         ],
-        compiler_params=local,
+        compiler_params=pltpu.CompilerParams(
+            collective_id=1, has_side_effects=True, vmem_limit_bytes=VMEM_LIMIT
+        ),
         name="coefficients",
-    )(vel, west, east, north, south, cwest, ceast, rbf, listed, lists)
+    )(vel, rbf, pos, bins, lists)
 
     out, land0, land1 = pl.pallas_call(
-        functools.partial(step_kernel, sizes, (bx, by), 20),
+        functools.partial(step_kernel, sizes, (bx, by), 2),
         out_shape=(
             jax.ShapeDtypeStruct((3, cap), f32),
             jax.ShapeDtypeStruct((3, count), f32),

time: 106 us -> 70.1 us (0.66)
  starting transfers between devices: 18.3 us -> 0 us
  Pallas kernels: 71.5 us -> 62.3 us
  waiting for transfers between devices: 5.25 us -> 0 us
  local copies, waits for them, and re-layouts: 8.32 us -> 6.65 us
  other arithmetic: 1.27 us -> 0 us
    ppermute x6 -> x0, starting transfers between devices: 18.3 us -> none  [shift(): lax.ppermute(block, axis, pairs if up else [(b, a) for a, b in pairs])]
    pallas_call x3 -> x2, Pallas kernels: 71.5 us -> 62.3 us  [the longest x1 31.6 us: body(): pl.pallas_call(functools.partial(coef_kernel, sizes), out_shape=(jax.Shap...]
    ppermute x6 -> x0, waiting for transfers between devices: 5.25 us -> none  [shift(): lax.ppermute(block, axis, pairs if up else [(b, a) for a, b in pairs])]
    slice x4 -> x0, local copies, waits for them, and re-layouts: 3.75 us -> none  [the longest x1 2.62 us: body(): east = shift(vel[:, :1], 'sub', False)]
    unnamed x23 -> x7, local copies, waits for them, and re-layouts: 2.36 us -> 4.81 us
    concatenate x2 -> x0, other arithmetic: 1.27 us -> none  [the longest x1 0.64 us: body(): jnp.concatenate([north[:, :1], south[:, :1]], axis=0)]
  transfers between devices with their start and end apart: 6 -> 0, of which waited for: 2 -> 0; matrix products, arithmetic and copies ran while one was open for 4% -> 0% of each run, Pallas kernels for 4% -> 0%
where the time goes in v1:
time: 70.1 us; the launch traced here: 69.6 us
  Pallas kernels  62.3 us (89%)
  local copies, waits for them, and re-layouts  6.65 us (9%)
  between operations  0.72 us (1%)
    pallas_call x1, Pallas kernels, body(): pl.pallas_call(functools.partial(coef_kernel, sizes), out_shape=(jax.Shap...  31.6 us
    pallas_call x1, Pallas kernels, body(): pl.pallas_call(functools.partial(step_kernel, sizes, (bx, by), 2), out_sh...  30.7 us
    unnamed x7, local copies, waits for them, and re-layouts  4.81 us
    dynamic_update_slice x2, local copies, waits for them, and re-layouts, body(): out = lax.dynamic_update_slice(out, land1, (jnp.int32(0), resident + count))  1.49 us

profile of v1, /device:TPU:1, one launch (start us, length us, event | category | flops | bytes accessed | tf_op | source)
XLA Modules:
  0.0 69.6 jit_solution(7359766908976934290)
XLA Ops:
  0.0 1.3 %copy.10 = f32[1,1,3,36864]{3,2,1,0:T(4,128)S(1)} copy(f32[1,1,3,36864]{3,1,2,0:T(1,128)} %param.8) | data formatting | bytes 884736
  1.3 0.0 copy-start
  1.3 1.9 %copy-done = f32[16,4,2,48,128]{4,3,2,1,0:T(8,128)S(1)} copy-done((f32[16,4,2,48,128]{4,3,2,1,0:T(8,128)S(1)}, f32[16,4,2,48,128]{4,3,2,1,0:T(8,128)}, u32[]{:S(2)}) %copy-start) | copy-done | bytes 3145752
  3.2 0.0 copy-start.1
  3.2 0.9 %copy-done.1 = s32[1,1,36864]{2,1,0:T(1,128)S(1)} copy-done((s32[1,1,36864]{2,1,0:T(1,128)S(1)}, s32[1,1,36864]{2,1,0:T(1,128)}, u32[]{:S(2)}) %copy-start.1) | copy-done | bytes 147480
  4.1 0.0 copy-start.2
  4.1 0.7 copy-done.2
  4.8 31.6 %coefficients.1 = (bf16[2,192,768]{2,1,0:T(8,128)(2,1)S(1)}, f32[8,8,128]{2,1,0:T(8,128)S(1)}, f32[3,1024]{1,0:T(4,128)S(1)}, f32[384,128]{1,0:T(8,128)S(1)}) custom-call(f32[16,4,96,128]{3,2,1,0:T(8,128)S(1)} %bitcast.17, f32[16,4,16,1152]{3,2,1,0:T(8,128)} %rbf.1, f32[3,36864]{1,0:T(4,128)S(1)} %bitcast.15, s32[1,36864]{1,0:T(1,128)S(1)} %bitcast.19, ...), custom_call_target="tpu_custom_call" | custom-call | tf_op jit(solution)/shard_map/coefficients/pallas_call | solution.py:390
  37.1 30.7 %advect.1 = (f32[3,36864]{1,0:T(4,128)S(1)}, f32[3,1024]{1,0:T(4,128)S(1)}, f32[3,1024]{1,0:T(4,128)S(1)}) custom-call(s32[1,1]{1,0:T(1,128)} %copy.13.live, f32[3,36864]{1,0:T(4,128)S(1)} %bitcast.16, s32[1,36864]{1,0:T(1,128)S(1)} %bitcast.20, f32[384,128]{1,0:T(8,128)S(1)} %get-tuple-element.12.gone, bf16[2,192,768]{2,1,0:T(8,128)(2,1)S(1)} %get-tuple-element.13.tab, ...), custom_call_target="tpu_custom_call" | custom-call | tf_op jit(solution)/shard_map/advect/pallas_call | solution.py:419
  67.8 0.3 dynamic_update_slice.8
  68.1 0.3 dynamic_update_slice.9
  68.4 1.2 %copy.7 = f32[1,1,3,36864]{3,1,2,0:T(1,128)} copy(f32[1,1,3,36864]{3,2,1,0:T(4,128)S(1)} %dynamic_update_slice.9) | data formatting | bytes 884736 | tf_op jit(solution)/shard_map/dynamic_update_slice | solution.py:445
  (1 shorter events, 0.0 us)
Async XLA Ops:
  1.3 1.9 %copy-start = (f32[16,4,2,48,128]{4,3,2,1,0:T(8,128)S(1)}, f32[16,4,2,48,128]{4,3,2,1,0:T(8,128)}, u32[]{:S(2)}) copy-start(f32[16,4,2,48,128]{4,3,2,1,0:T(8,128)} %param.6) | copy-start | bytes 9437188
  3.2 0.9 %copy-start.1 = (s32[1,1,36864]{2,1,0:T(1,128)S(1)}, s32[1,1,36864]{2,1,0:T(1,128)}, u32[]{:S(2)}) copy-start(s32[1,1,36864]{2,1,0:T(1,128)} %param.9) | copy-start | bytes 442372
  4.1 0.7 %copy-start.2 = (s32[1,1,2,8,128]{4,3,2,1,0:T(8,128)S(1)}, s32[1,1,2,8,128]{4,3,2,1,0:T(8,128)}, u32[]{:S(2)}) copy-start(s32[1,1,2,8,128]{4,3,2,1,0:T(8,128)} %param.11) | copy-start | bytes 24580

commit v2 on v1

--- a/solution.py
+++ b/solution.py
@@ -11,7 +11,7 @@
 MIG = 128
 LANES = 128
 CHUNK = 1024
-BULK = 4096
+PARTS = 8
 
 time_step = 0.1
 compass = ((-1, -1), (-1, 0), (-1, 1), (0, -1), (0, 1), (1, -1), (1, 0), (1, 1))
@@ -19,7 +19,7 @@
 MESH = pl.DeviceIdType.MESH
 f32 = jnp.float32
 bf16 = jnp.bfloat16
-VMEM_LIMIT = 48 * 2**20
+VMEM_LIMIT = 56 * 2**20
 
 
 def halves(v):
@@ -72,16 +72,16 @@
 
 
 def gather_lists(pos_ref, bins_ref, list_ref, listed_ref, gone_ref, rows):
-    count = pos_ref.shape[1] // LANES
+    count = bins_ref.shape[1] // LANES
     padded = rows.shape[1]
     if padded > count:
         rows[:, count:, :] = jnp.zeros((4, padded - count, LANES), f32)
 
     def fold(q, carry):
         at = pl.ds(pl.multiple_of(q * LANES, LANES), LANES)
-        v = pos_ref[:, at]
         for k in range(3):
-            rows[k, pl.ds(q, 1), :] = v[k : k + 1]
+            there = pl.ds(pl.multiple_of((k * count + q) * LANES, LANES), LANES)
+            rows[k, pl.ds(q, 1), :] = pos_ref[:, there]
         rows[3, pl.ds(q, 1), :] = bins_ref[:, at].astype(f32)
         return carry
 
@@ -128,11 +128,15 @@
 
 
 def coef_kernel(
-    sizes, vel, rbf, pos, bins, lists, tab, pay, fin, gone,
-    west, east, north, south, corners, acc, tabf, listed, folded, send, recv,
+    sizes, vel_far, rbf_far, pos, bins, lists, tab, pay, fin, gone,
+    vel, rbf, west, east, north, south, corners, acc, tabf, listed, folded, send, recv, near,
 ):
     bx, by = vel.shape[0], vel.shape[1]
     blocks = bx * by
+    fetches = [
+        pltpu.make_async_copy(vel_far, vel, near.at[0]),
+        pltpu.make_async_copy(rbf_far, rbf, near.at[1]),
+    ]
     present, target = grid_peers(sizes)
     for box in (west, east, north, south, corners):
         box[...] = jnp.zeros(box.shape, f32)
@@ -144,11 +148,11 @@
         row_at = 0 if dr < 0 else bx - 1
         col_at = 0 if dc < 0 else by - 1
         if dr == 0:
-            src = vel.at[:, col_at]
+            src = vel_far.at[:, col_at]
         elif dc == 0:
-            src = vel.at[row_at]
+            src = vel_far.at[row_at]
         else:
-            src = vel.at[row_at, col_at]
+            src = vel_far.at[row_at, col_at]
         return pltpu.make_async_remote_copy(
             src_ref=src, dst_ref=boxes[7 - e], send_sem=send.at[e], recv_sem=recv.at[7 - e],
             device_id=target(e), device_id_type=MESH,
@@ -159,6 +163,8 @@
         def _():
             halo(e).start()
 
+    for fetch in fetches:
+        fetch.start()
     gather_lists(pos, bins, lists, listed, gone, folded)
     acc[...] = jnp.zeros(acc.shape, f32)
 
@@ -197,6 +203,8 @@
         row(lambda j: west[i] if j < 0 else east[i], around(i), (-1, by))
         return carry
 
+    for fetch in fetches:
+        fetch.wait()
     lax.fori_loop(0, bx, inner, 0)
     for e in range(8):
         @pl.when(present(e))
@@ -259,7 +267,7 @@
 
 def step_kernel(
     sizes, shape, split, live, pos, bins, gone, tab, pay, fin, leaving,
-    out, land0, land1, box0, box1, pay1, spread, send0, recv0, send1, recv1,
+    out, land, box0, box1, pay1, spread, send0, recv0, send1, recv1,
 ):
     bx, by = shape
     blocks = bx * by
@@ -291,16 +299,22 @@
                 parcel(7 - d, src, box, send, recv).wait_recv()
 
     resident = live[0, 0]
+    cap = bins.shape[1]
+    arrivals = 8 * MIG
+    most = cap - 2 * arrivals
+    width = most // PARTS
+    for k in range(3):
+        out[:, k * cap + most : (k + 1) * cap] = jnp.zeros((1, cap - most), f32)
 
     def bulk(i, carry):
-        at = pl.ds(pl.multiple_of(i * BULK, BULK), BULK)
-        slot = lax.broadcasted_iota(jnp.int32, (1, BULK), 1) + i * BULK
+        at = pl.ds(pl.multiple_of(i * width, LANES), width)
+        slot = lax.broadcasted_iota(jnp.int32, (1, width), 1) + i * width
         alive = slot < resident
-        v = jnp.where(alive, pos[:, at], 0.0)
-        x, y, z = v[0:1], v[1:2], v[2:3]
+        ats = [pl.ds(pl.multiple_of(k * cap + i * width, LANES), width) for k in range(3)]
+        x, y, z = [jnp.where(alive, pos[:, there], 0.0) for there in ats]
         n = bins[:, at]
         left = jnp.concatenate(
-            [gone[pl.ds(i * (BULK // LANES) + k, 1), :] for k in range(BULK // LANES)], axis=1
+            [gone[pl.ds(i * (width // LANES) + k, 1), :] for k in range(width // LANES)], axis=1
         )
         ax, ay = anchors(n, by)
         hot = hot_rows(blocks, n).astype(bf16)
@@ -309,7 +323,7 @@
         u = velocity_at(mx, my, mz, ax, ay, hot, tab[1])
         keep = alive & (left == 0.0)
         for k, (p, q) in enumerate(zip((x, y, z), u)):
-            out[k : k + 1, at] = jnp.where(keep, p + time_step * q, 0.0)
+            out[:, ats[k]] = jnp.where(keep, p + time_step * q, 0.0)
         return carry
 
     post(pay, box0, send0, recv0)
@@ -330,7 +344,8 @@
         living.append(rows[7])
         for k in range(3):
             f = rows[k] + time_step * u[k]
-            land0[k : k + 1, c * CHUNK : (c + 1) * CHUNK] = f
+            begin = 2 * k * arrivals + c * CHUNK
+            land[:, begin : begin + CHUNK] = f
             for e in range(per):
                 spread[c * per + e : c * per + e + 1, k * LANES : (k + 1) * LANES] = f[
                     :, e * LANES : (e + 1) * LANES
@@ -366,12 +381,15 @@
         sl = slice(d * MIG, (d + 1) * MIG)
         stays = jnp.where(left[d : d + 1] == 0.0, 1.0, 0.0)
         stays = stays * living[d // per][:, (d % per) * MIG : (d % per + 1) * MIG]
-        land0[:, sl] = land0[:, sl] * stays
-    lax.fori_loop(split, pos.shape[1] // BULK, bulk, 0)
+        for k in range(3):
+            begin = 2 * k * arrivals + d * MIG
+            land[:, begin : begin + MIG] = land[:, begin : begin + MIG] * stays
+    lax.fori_loop(split, PARTS, bulk, 0)
     collect(pay1, box1, send1, recv1)
     for d in range(8):
         for k in range(3):
-            land1[k : k + 1, d * MIG : (d + 1) * MIG] = box1[d, k : k + 1, :] * box1[d, 3:4, :]
+            begin = (2 * k + 1) * arrivals + d * MIG
+            land[:, begin : begin + MIG] = box1[d, k : k + 1, :] * box1[d, 3:4, :]
 
 
 def body(sizes, velocity, rbf_coef, positions, cell_bins, live_count, departures):
@@ -380,7 +398,7 @@
     count = 8 * MIG
     vel = velocity.reshape(bx, by, 2 * c3l, cb)
     rbf = rbf_coef
-    pos = positions[0, 0]
+    pos = positions.reshape(1, 3 * cap)
     bins = cell_bins.reshape(1, cap)
     lists = departures.reshape(1, 2 * count)
     vmem = pl.BlockSpec(memory_space=pltpu.VMEM)
@@ -395,9 +413,11 @@
             jax.ShapeDtypeStruct((3, count), f32),
             jax.ShapeDtypeStruct((rows, LANES), f32),
         ),
-        in_specs=[vmem] * 5,
+        in_specs=[pl.BlockSpec(memory_space=pl.ANY)] * 2 + [vmem] * 3,
         out_specs=(vmem,) * 4,
         scratch_shapes=[
+            pltpu.VMEM(vel.shape, f32),
+            pltpu.VMEM(rbf.shape, f32),
             pltpu.VMEM((bx, 2 * c3l, cb), f32),
             pltpu.VMEM((bx, 2 * c3l, cb), f32),
             pltpu.VMEM((by, 2 * c3l, cb), f32),
@@ -409,6 +429,7 @@
             pltpu.VMEM((4, rows, LANES), f32),
             pltpu.SemaphoreType.DMA((8,)),
             pltpu.SemaphoreType.DMA((8,)),
+            pltpu.SemaphoreType.DMA((2,)),
         ],
         compiler_params=pltpu.CompilerParams(
             collective_id=1, has_side_effects=True, vmem_limit_bytes=VMEM_LIMIT
@@ -416,15 +437,14 @@
         name="coefficients",
     )(vel, rbf, pos, bins, lists)
 
-    out, land0, land1 = pl.pallas_call(
+    out, land = pl.pallas_call(
         functools.partial(step_kernel, sizes, (bx, by), 2),
         out_shape=(
-            jax.ShapeDtypeStruct((3, cap), f32),
-            jax.ShapeDtypeStruct((3, count), f32),
-            jax.ShapeDtypeStruct((3, count), f32),
+            jax.ShapeDtypeStruct((1, 3 * cap), f32),
+            jax.ShapeDtypeStruct((1, 6 * count), f32),
         ),
         in_specs=[smem] + [vmem] * 7,
-        out_specs=(vmem,) * 3,
+        out_specs=(vmem,) * 2,
         scratch_shapes=[
             pltpu.VMEM((8, 8, MIG), f32),
             pltpu.VMEM((8, 8, MIG), f32),
@@ -441,9 +461,10 @@
         name="advect",
     )(live_count, pos, bins, gone, tab, pay, fin, lists[:, count:])
     resident = live_count[0, 0]
-    out = lax.dynamic_update_slice(out, land0, (jnp.int32(0), resident))
-    out = lax.dynamic_update_slice(out, land1, (jnp.int32(0), resident + count))
-    return out[None, None]
+    for k in range(3):
+        piece = land[:, 2 * count * k : 2 * count * (k + 1)]
+        out = lax.dynamic_update_slice(out, piece, (jnp.int32(0), k * cap + resident))
+    return out.reshape(1, 1, 3, cap)
 
 
 def solution(mesh):

time: 70.1 us -> 70.6 us (level)
  local copies, waits for them, and re-layouts: 6.65 us -> 7.84 us
    unnamed x7 -> x3, local copies, waits for them, and re-layouts: 4.81 us -> 1.81 us
    dynamic_update_slice x3, local copies, waits for them, and re-layouts: 1.84 us -> 4.7 us  [body(): lax.dynamic_update_slice(out, piece, (jnp.int32(0), k * cap + resident))]
    slice x0 -> x1, local copies, waits for them, and re-layouts: none -> 0.73 us  [body(): piece = land[:, 2 * count * k:2 * count * (k + 1)]]
where the time goes in v2:
time: 70.6 us; the launch traced here: 70.1 us
  Pallas kernels  61.6 us (87%)
  local copies, waits for them, and re-layouts  7.84 us (11%)
    pallas_call x1, Pallas kernels, body(): pl.pallas_call(functools.partial(coef_kernel, sizes), out_shape=(jax.Shap...  31.2 us
    pallas_call x1, Pallas kernels, body(): pl.pallas_call(functools.partial(step_kernel, sizes, (bx, by), 2), out_sh...  30.4 us
    dynamic_update_slice x3, local copies, waits for them, and re-layouts, body(): lax.dynamic_update_slice(out, piece, (jnp.int32(0), k * cap + resident))  4.7 us
    unnamed x3, local copies, waits for them, and re-layouts  1.81 us

profile of v2, /device:TPU:1, one launch (start us, length us, event | category | flops | bytes accessed | tf_op | source)
XLA Modules:
  0.0 70.1 jit_solution(18182455179217820204)
XLA Ops:
  0.0 0.0 copy-start
  0.7 31.2 %coefficients.1 = (bf16[2,192,768]{2,1,0:T(8,128)(2,1)}, f32[8,8,128]{2,1,0:T(8,128)}, f32[3,1024]{1,0:T(4,128)}, f32[384,128]{1,0:T(8,128)}) custom-call(f32[16,4,96,128]{3,2,1,0:T(8,128)} %bitcast.13, f32[16,4,16,1152]{3,2,1,0:T(8,128)} %rbf_far.1, f32[1,110592]{1,0:T(1,128)} %bitcast.14, s32[1,36864]{1,0:T(1,128)} %bitcast.16, s32[1,2048]{1,0:T(1,128)} %bitcast.19), custom_call_target="tpu_custom_call" | custom-call | tf_op jit(solution)/shard_map/coefficients/pallas_call | solution.py:408
  31.9 0.0 copy-done
  31.9 0.6 slice.16.leaving
  32.5 30.4 %advect.1 = (f32[1,110592]{1,0:T(1,128)}, f32[1,6144]{1,0:T(1,128)}) custom-call(s32[1,1]{1,0:T(1,128)} %copy.13.live, f32[1,110592]{1,0:T(1,128)} %bitcast.15, s32[1,36864]{1,0:T(1,128)} %bitcast.17, f32[384,128]{1,0:T(8,128)} %get-tuple-element.11.gone, bf16[2,192,768]{2,1,0:T(8,128)(2,1)} %get-tuple-element.12.tab, f32[8,8,128]{2,1,0:T(8,128)} %get-tuple-element.13.pay, ...), custom_call_target="tpu_custom_call" | custom-call | tf_op jit(solution)/shard_map/advect/pallas_call | solution.py:440
  62.9 0.7 %fusion = (f32[1,2048]{1,0:T(1,128)S(1)}, f32[1,2048]{1,0:T(1,128)S(1)}, f32[1,2048]{1,0:T(1,128)S(1)}) fusion(f32[1,6144]{1,0:T(1,128)} %get-tuple-element.16), kind=kLoop, calls=%fused_computation | loop fusion | bytes 49152 | tf_op jit(solution)/shard_map/slice | solution.py:465
  63.6 1.6 %dynamic_update_slice.9 = f32[1,110592]{1,0:T(1,128)} dynamic-update-slice(f32[1,110592]{1,0:T(1,128)} %get-tuple-element.15, f32[1,2048]{1,0:T(1,128)S(1)} %get-tuple-element.19, s32[]{:T(128)} %constant.2.clone.1, s32[]{:T(128)S(6)} %select_n.9) | dynamic-update-slice | bytes 16388 | tf_op jit(solution)/shard_map/dynamic_update_slice | solution.py:466
  65.2 1.6 %dynamic_update_slice.10 = f32[1,110592]{1,0:T(1,128)} dynamic-update-slice(f32[1,110592]{1,0:T(1,128)} %dynamic_update_slice.9, f32[1,2048]{1,0:T(1,128)S(1)} %get-tuple-element.18, s32[]{:T(128)} %constant.2.clone.1, s32[]{:T(128)S(6)} %select_n.10) | dynamic-update-slice | bytes 16388 | tf_op jit(solution)/shard_map/dynamic_update_slice | solution.py:466
  66.7 1.6 %dynamic_update_slice.11 = f32[1,110592]{1,0:T(1,128)} dynamic-update-slice(f32[1,110592]{1,0:T(1,128)} %dynamic_update_slice.10, f32[1,2048]{1,0:T(1,128)S(1)} %get-tuple-element.17, s32[]{:T(128)} %constant.2.clone.1, s32[]{:T(128)S(6)} %select_n.11) | dynamic-update-slice | bytes 16388 | tf_op jit(solution)/shard_map/dynamic_update_slice | solution.py:466
  68.3 1.8 %copy.14 = f32[1,1,3,36864]{3,1,2,0:T(1,128)} copy(f32[1,1,3,36864]{3,1,2,0:T(1,128)} %bitcast.18) | data formatting | bytes 884736
Async XLA Ops:
  0.0 31.9 %copy-start = (s32[1,1,2,8,128]{4,3,2,1,0:T(8,128)S(1)}, s32[1,1,2,8,128]{4,3,2,1,0:T(8,128)}, u32[]{:S(2)}) copy-start(s32[1,1,2,8,128]{4,3,2,1,0:T(8,128)} %param.11) | copy-start | bytes 24580

commit v3 on v2

--- a/solution.py
+++ b/solution.py
@@ -303,8 +303,7 @@
     arrivals = 8 * MIG
     most = cap - 2 * arrivals
     width = most // PARTS
-    for k in range(3):
-        out[:, k * cap + most : (k + 1) * cap] = jnp.zeros((1, cap - most), f32)
+    out[:, most:] = jnp.zeros((3, cap - most), f32)
 
     def bulk(i, carry):
         at = pl.ds(pl.multiple_of(i * width, LANES), width)
@@ -323,7 +322,7 @@
         u = velocity_at(mx, my, mz, ax, ay, hot, tab[1])
         keep = alive & (left == 0.0)
         for k, (p, q) in enumerate(zip((x, y, z), u)):
-            out[:, ats[k]] = jnp.where(keep, p + time_step * q, 0.0)
+            out[k : k + 1, at] = jnp.where(keep, p + time_step * q, 0.0)
         return carry
 
     post(pay, box0, send0, recv0)
@@ -344,14 +343,13 @@
         living.append(rows[7])
         for k in range(3):
             f = rows[k] + time_step * u[k]
-            begin = 2 * k * arrivals + c * CHUNK
-            land[:, begin : begin + CHUNK] = f
+            land[k : k + 1, c * CHUNK : (c + 1) * CHUNK] = f
             for e in range(per):
                 spread[c * per + e : c * per + e + 1, k * LANES : (k + 1) * LANES] = f[
                     :, e * LANES : (e + 1) * LANES
                 ]
 
-    slots = leaving[...]
+    slots = leaving[:, arrivals:]
     flags = jnp.where(slots >= 0, 1.0, 0.0)
     late = slots >= resident
     rel = jnp.where(late & (slots >= 0), slots - resident, -1)
@@ -381,15 +379,13 @@
         sl = slice(d * MIG, (d + 1) * MIG)
         stays = jnp.where(left[d : d + 1] == 0.0, 1.0, 0.0)
         stays = stays * living[d // per][:, (d % per) * MIG : (d % per + 1) * MIG]
-        for k in range(3):
-            begin = 2 * k * arrivals + d * MIG
-            land[:, begin : begin + MIG] = land[:, begin : begin + MIG] * stays
+        land[:, sl] = land[:, sl] * stays
     lax.fori_loop(split, PARTS, bulk, 0)
     collect(pay1, box1, send1, recv1)
     for d in range(8):
         for k in range(3):
-            begin = (2 * k + 1) * arrivals + d * MIG
-            land[:, begin : begin + MIG] = box1[d, k : k + 1, :] * box1[d, 3:4, :]
+            begin = arrivals + d * MIG
+            land[k : k + 1, begin : begin + MIG] = box1[d, k : k + 1, :] * box1[d, 3:4, :]
 
 
 def body(sizes, velocity, rbf_coef, positions, cell_bins, live_count, departures):
@@ -440,8 +436,8 @@
     out, land = pl.pallas_call(
         functools.partial(step_kernel, sizes, (bx, by), 2),
         out_shape=(
-            jax.ShapeDtypeStruct((1, 3 * cap), f32),
-            jax.ShapeDtypeStruct((1, 6 * count), f32),
+            jax.ShapeDtypeStruct((3, cap), f32),
+            jax.ShapeDtypeStruct((3, 2 * count), f32),
         ),
         in_specs=[smem] + [vmem] * 7,
         out_specs=(vmem,) * 2,
@@ -459,12 +455,9 @@
             collective_id=0, has_side_effects=True, vmem_limit_bytes=VMEM_LIMIT
         ),
         name="advect",
-    )(live_count, pos, bins, gone, tab, pay, fin, lists[:, count:])
+    )(live_count, pos, bins, gone, tab, pay, fin, lists)
     resident = live_count[0, 0]
-    for k in range(3):
-        piece = land[:, 2 * count * k : 2 * count * (k + 1)]
-        out = lax.dynamic_update_slice(out, piece, (jnp.int32(0), k * cap + resident))
-    return out.reshape(1, 1, 3, cap)
+    return lax.dynamic_update_slice(out, land, (jnp.int32(0), resident))[None, None]
 
 
 def solution(mesh):

time: 70.6 us -> 66.4 us (0.941)
  local copies, waits for them, and re-layouts: 7.84 us -> 3.72 us
    unnamed x3 -> x0, local copies, waits for them, and re-layouts: 1.81 us -> none
    slice x2 -> x0, local copies, waits for them, and re-layouts: 1.33 us -> none  [the longest x1 0.73 us: body(): piece = land[:, 2 * count * k:2 * count * (k + 1)]]
    dynamic_update_slice x3 -> x2, local copies, waits for them, and re-layouts: 4.7 us -> 3.72 us  [body(): lax.dynamic_update_slice(out, land, (jnp.int32(0), resident))[None, None]]
where the time goes in v3:
time: 66.4 us; the launch traced here: 66 us
  Pallas kernels  61.6 us (93%)
  local copies, waits for them, and re-layouts  3.72 us (6%)
  between operations  0.67 us (1%)
    pallas_call x1, Pallas kernels, body(): pl.pallas_call(functools.partial(coef_kernel, sizes), out_shape=(jax.Shap...  31.2 us
    pallas_call x1, Pallas kernels, body(): pl.pallas_call(functools.partial(step_kernel, sizes, (bx, by), 2), out_sh...  30.4 us
    dynamic_update_slice x2, local copies, waits for them, and re-layouts, body(): lax.dynamic_update_slice(out, land, (jnp.int32(0), resident))[None, None]  3.72 us

profile of v3, /device:TPU:1, one launch (start us, length us, event | category | flops | bytes accessed | tf_op | source)
XLA Modules:
  0.0 66.0 jit_solution(7200112348462169174)
XLA Ops:
  0.0 31.2 %coefficients.1 = (bf16[2,192,768]{2,1,0:T(8,128)(2,1)}, f32[8,8,128]{2,1,0:T(8,128)}, f32[3,1024]{1,0:T(4,128)}, f32[384,128]{1,0:T(8,128)}) custom-call(f32[16,4,96,128]{3,2,1,0:T(8,128)} %bitcast.10, f32[16,4,16,1152]{3,2,1,0:T(8,128)} %rbf_far.1, f32[1,110592]{1,0:T(1,128)} %bitcast.11, s32[1,36864]{1,0:T(1,128)} %bitcast.14, s32[1,2048]{1,0:T(1,128)} %bitcast.16), custom_call_target="tpu_custom_call" | custom-call | tf_op jit(solution)/shard_map/coefficients/pallas_call | solution.py:404
  31.8 30.4 %advect.1 = (f32[3,36864]{1,0:T(4,128)}, f32[3,2048]{1,0:T(4,128)}) custom-call(s32[1,1]{1,0:T(1,128)} %copy.9.live, f32[1,110592]{1,0:T(1,128)} %bitcast.12, s32[1,36864]{1,0:T(1,128)} %bitcast.15, f32[384,128]{1,0:T(8,128)} %get-tuple-element.11.gone, bf16[2,192,768]{2,1,0:T(8,128)(2,1)} %get-tuple-element.12.tab, f32[8,8,128]{2,1,0:T(8,128)} %get-tuple-element.13.pay, ...), custom_call_target="tpu_custom_call" | custom-call | tf_op jit(solution)/shard_map/advect/pallas_call | solution.py:436
  62.3 1.4 %dynamic_update_slice.4 = f32[1,1,3,36864]{3,2,1,0:T(4,128)} dynamic-update-slice(f32[1,1,3,36864]{3,2,1,0:T(4,128)} %bitcast.13, f32[1,1,3,2048]{3,2,1,0:T(4,128)} %bitcast.18, s32[]{:T(128)} %constant.1.clone.1, s32[]{:T(128)} %constant.1.clone.1, s32[]{:T(128)} %constant.1.clone.1, s32[]{:T(128)S(6)} %select_n.3) | dynamic-update-slice | bytes 49156 | tf_op jit(solution)/shard_map/dynamic_update_slice | solution.py:460
  63.7 2.3 %copy.7 = f32[1,1,3,36864]{3,1,2,0:T(1,128)} copy(f32[1,1,3,36864]{3,2,1,0:T(4,128)} %dynamic_update_slice.4) | data formatting | bytes 884736 | tf_op jit(solution)/shard_map/dynamic_update_slice | solution.py:460
